TPU v7x, 256 devices: a whole 4x4x8 slice. The times are simulated.
256 devices in a mesh: view: 2 (over core), row: 16 (over x, y), feat: 8 (over z).
Axes of the slice: x: 4, y: 4, z: 8, core: 2. Of those that a mesh axis runs over, the one named last changes fastest.
Arguments:
- views: bfloat16 [2, 98304, 4096], P('view', ('row', 'feat')), may hold values from -8 to 8
- weights: float32 [2, 4096, 256], P('view', ('row', 'feat')), may hold values from -6 to 6
Outputs:
- new_weights: float32 [2, 4096, 256], P('view', ('row', 'feat'))
- projected: bfloat16 [2, 98304, 256], P('view', ('row', 'feat'))
All inputs are finite; a program needn't handle non-finite values.
Results may differ from a plain program's by a relative error of at most 0.012.
Values may be sent and summed in bfloat16 or wider, within the bound.
A program may use at most 64 MiB of HBM per device.

v0:
```python
import math

import jax
import jax.numpy as jnp
from jax import lax
from jax.sharding import PartitionSpec as P

ITERS = 2


epsilon = 1e-06
step_rate = 0.5


def swapped(block, axis, distance):
    count = lax.axis_size(axis)
    route = []
    for low in range(count):
        high = low | 1 << distance
        if high != low and high < count:
            route += [(low, high), (high, low)]
    return lax.ppermute(block, axis, route)


def on_device(views, weights):
    samples = views[0]
    own_rows = weights[0]
    rows_here = samples.shape[0]
    row_total = rows_here * lax.axis_size("row") * lax.axis_size("feat")
    width_root = math.sqrt(samples.shape[1])
    shown = None
    for sweep in range(ITERS):
        halved = own_rows.astype(jnp.bfloat16)
        whole_dirs = lax.all_gather(halved, ("row", "feat"), axis=0, tiled=True)
        summed_proj = jnp.dot(samples, whole_dirs, preferred_element_type=jnp.float32)
        squares = jnp.sum(summed_proj * summed_proj, axis=0)
        col_sums = lax.psum(squares, ("row", "feat"))
        scaling = lax.rsqrt(col_sums / row_total + epsilon)
        own_proj = (summed_proj * scaling).astype(jnp.bfloat16)
        partner_proj = swapped(own_proj, "view", 0)
        residue = (own_proj.astype(jnp.float32) - partner_proj.astype(jnp.float32)).astype(
            jnp.bfloat16
        )
        grad_share = lax.psum_scatter(
            lax.dot_general(
                samples, residue, (((0,), (0,)), ((), ())), preferred_element_type=jnp.float32
            ),
            ("row", "feat"),
            scatter_dimension=0,
            tiled=True,
        )
        own_rows = width_root * (own_rows * scaling - step_rate * (grad_share / row_total))
        shown = own_proj
    return (own_rows[None], shown[None])


def solution(mesh):
    in_specs = (P("view", ("row", "feat"), None), P("view", ("row", "feat"), None))
    out_specs = (P("view", ("row", "feat"), None), P("view", ("row", "feat"), None))
    return jax.shard_map(
        on_device, mesh=mesh, in_specs=in_specs, out_specs=out_specs, check_vma=False
    )
```

profile of v0, /device:TPU:0, one launch (start us, length us, event | category | flops | bytes accessed | tf_op | source)
XLA Modules:
  0.0 2366.0 jit_solution(5700873499439995862)
XLA Ops:
  7.2 0.0 all-gather.3.cloned.1.call-start
  7.2 1.4 bitcast_convert_fusion
  8.6 0.0 all-gather.3.cloned.1.call-update
  8.6 0.0 reduce-scatter.7.cloned.1.call-start
  8.7 119.0 %all-gather.3.cloned.1.call-done = bf16[4096,256]{1,0:T(8,128)(2,1)} async-done(((bf16[32,256]{1,0:T(8,128)(2,1)}), bf16[4096,256]{1,0:T(8,128)(2,1)}) %all-gather.3.cloned.1.call-update) | async-done | bytes 2097168 | tf_op jit(solution)/shard_map/all_gather | solution.py:34
  127.7 5.2 multiply_reduce_fusion.1
  132.9 346.7 %psum.14 = f32[256]{0:T(256)S(1)} all-reduce(f32[256]{0:T(256)S(1)} %get-tuple-element.8), channel_id=1, replica_groups=mesh['view'=2,'row'=16,'feat'=8] {'row','feat'}, use_global_device_ids=true, to_apply=%region_1.0 | all-reduce | flops 256 | bytes 2048 | tf_op jit(solution)/shard_map/psum | solution.py:37
  479.6 0.1 multiply_convert_fusion.1
  479.7 0.1 collective-permute-start
  479.8 1.7 collective-permute-done
  481.5 6.6 fusion.8
  488.1 5.6 copy.10
  493.7 0.0 copy-start
  493.7 0.0 reduce-scatter.7.cloned.1.call-update
  493.7 0.0 all-gather.5.cloned.1.call-start
  493.7 693.1 %reduce-scatter.7.cloned.1.call-done = f32[32,256]{1,0:T(8,128)} async-done(((f32[4096,256]{1,0:T(8,128)}), f32[32,256]{1,0:T(8,128)}) %reduce-scatter.7.cloned.1.call-update) | async-done | bytes 32784 | tf_op jit(solution)/shard_map/reduce_scatter | solution.py:44
  1186.8 0.0 copy-done
  1186.8 1.4 multiply_convert_fusion.2
  1188.2 0.0 all-gather.5.cloned.1.call-update
  1188.2 0.0 reduce-scatter.9.cloned.1.call-start
  1188.3 109.8 %all-gather.5.cloned.1.call-done = bf16[4096,256]{1,0:T(8,128)(2,1)} async-done(((bf16[32,256]{1,0:T(8,128)(2,1)}), bf16[4096,256]{1,0:T(8,128)(2,1)}) %all-gather.5.cloned.1.call-update) | async-done | bytes 2097168 | tf_op jit(solution)/shard_map/all_gather | solution.py:34
  1298.1 5.3 multiply_reduce_fusion
  1303.4 346.7 %psum.15 = f32[256]{0:T(256)S(1)} all-reduce(f32[256]{0:T(256)S(1)} %get-tuple-element.10), channel_id=1, replica_groups=mesh['view'=2,'row'=16,'feat'=8] {'row','feat'}, use_global_device_ids=true, to_apply=%region_4.0 | all-reduce | flops 256 | bytes 2048 | tf_op jit(solution)/shard_map/psum | solution.py:37
  1650.1 0.1 fusion.19
  1650.2 0.1 collective-permute-start.1
  1650.3 1.7 collective-permute-done.1
  1652.0 6.6 fusion.11
  1658.6 5.6 copy.12
  1664.2 0.0 copy-start.1
  1664.2 0.0 reduce-scatter.9.cloned.1.call-update
  1664.3 0.1 fusion.18
  1664.4 0.9 copy.9
  1665.3 692.8 %reduce-scatter.9.cloned.1.call-done = f32[32,256]{1,0:T(8,128)} async-done(((f32[4096,256]{1,0:T(8,128)}), f32[32,256]{1,0:T(8,128)}) %reduce-scatter.9.cloned.1.call-update) | async-done | bytes 32784 | tf_op jit(solution)/shard_map/reduce_scatter | solution.py:44
  2358.1 0.0 copy-done.1
  2358.1 1.4 multiply_bitcast_fusion
  (2 shorter events, 0.0 us)
Async XLA Ops:
  7.2 120.5 %all-gather.3.cloned.1.call-start = ((), (), s32[]{:S(2)}) async-start(), calls=%async_computation.2 | async-start | bytes 2113536 | tf_op jit(solution)/shard_map/all_gather | solution.py:34
  8.6 1178.2 %reduce-scatter.7.cloned.1.call-start = ((), (), s32[]{:S(2)}) async-start(), calls=%async_computation.4 | async-start | bytes 4227072 | tf_op jit(solution)/shard_map/reduce_scatter | solution.py:44
  479.7 1.8 collective-permute-start
  493.7 693.2 %copy-start = (f32[1,32,256]{2,1,0:T(8,128)S(1)}, f32[1,32,256]{2,1,0:T(8,128)}, u32[]{:S(2)}) copy-start(f32[1,32,256]{2,1,0:T(8,128)} %param.3) | copy-start | bytes 98308
  493.7 804.4 %all-gather.5.cloned.1.call-start = ((), (), s32[]{:S(2)}) async-start(), calls=%async_computation.3 | async-start | bytes 2113536 | tf_op jit(solution)/shard_map/all_gather | solution.py:34
  1188.2 1169.9 %reduce-scatter.9.cloned.1.call-start = ((), (), s32[]{:S(2)}) async-start(), calls=%async_computation.5 | async-start | bytes 4227072 | tf_op jit(solution)/shard_map/reduce_scatter | solution.py:44
  1650.2 1.8 collective-permute-start.1
  1664.2 693.9 %copy-start.1 = (f32[32,256]{1,0:T(8,128)S(1)}, f32[32,256]{1,0:T(8,128)}, u32[]{:S(2)}) copy-start(f32[32,256]{1,0:T(8,128)} %reduce-scatter.7.cloned.1.call-done) | copy-start | bytes 98308
Sparse Core Ops, SparseCore 0:
  12.3 115.3 all-gather.2
  493.8 692.9 reduce-scatter.6
  1191.8 106.2 all-gather.4
  1664.4 693.6 reduce-scatter.8
where the time goes:
time: 2370 us
  waiting for transfers between devices  1620 us (68%)
  blocking collectives  693 us (29%)
  matrix products  23.8 us (1%)
    reduce_scatter x2, waiting for transfers between devices, on_device(): lax.psum_scatter(lax.dot_general(samples, residue, (((0,), (0,)), ((), ()...  1390 us
    psum x2, blocking collectives, on_device(): col_sums = lax.psum(squares, ('row', 'feat'))  693 us
    all_gather x2, waiting for transfers between devices, on_device(): whole_dirs = lax.all_gather(halved, ('row', 'feat'), axis=0, tiled=True)  229 us
  transfers between devices with their start and end apart: 6, of which 6 were waited for; matrix products, arithmetic and copies ran while one was open for 0% of the time, Pallas kernels for 0%

commit v1 on v0

v1 whole, which is shorter than its diff:
```python
import functools
import math

import jax
import jax.numpy as jnp
from jax import lax
from jax.experimental import pallas as pl
from jax.experimental.pallas import tpu as pltpu
from jax.sharding import PartitionSpec as P

ITERS = 2
EPSILON = 1e-06
STEP_RATE = 0.5
LANES = 256
PIECE = 16
MESH = pl.DeviceIdType.MESH


def layout(n, nz):
    sizes = {
        "gz": 2 * nz,
        "gm": 4 * n,
        "gl": 4 * n * n,
        "n1": n * n,
        "n2": 2 * nz,
        "swap": 1,
        "r1": 4 * n * n,
        "r2": 4 * n,
        "r3": nz,
    }
    start, places = 0, {}
    for name, count in sizes.items():
        places[name] = start
        start += count
    return places, start


def ring_order(nz):
    return sorted(range(nz), key=lambda d: (min(d, nz - d), d))


def kernel(dims, total_rows, root, x_hbm, w_hbm, wout_ref, proj_ref, *scratch):
    n, nz = dims
    (xs, w_in, perm, xp, xt, wg, pf, pp, rr, n1, n2, gs, r1, t2, r2, t3, r3,
     own_w, send_sem, recv_sem, load_sem) = scratch
    rows, feats = xs.shape
    blocks = own_w.shape[0]
    near = nz // 2
    offs = ring_order(nz)
    places, _ = layout(n, nz)
    strip = nz * 2 * PIECE
    span = near * PIECE
    others = sorted(range(1, n), key=lambda d: (min(d, n - d), d))
    by_m = others + [0]

    v = lax.axis_index("view")
    r = lax.axis_index("row")
    z = lax.axis_index("feat")
    x, y = r // n, lax.rem(r, n)

    def ahead(i, d, size):
        return lax.rem(i + d, size) if d else i

    def device(dv, dx, dy, dz):
        return (ahead(v, dv, 2), ahead(x, dx, n) * n + ahead(y, dy, n), ahead(z, dz, nz))

    def along_l(p, d):
        return (0, d, 0, 0) if p == 0 else (0, 0, d, 0)

    def along_m(p, d):
        return (0, 0, d, 0) if p == 0 else (0, d, 0, 0)

    partners = [(0, dx, dy, 0) for dx in range(n) for dy in range(n) if dx or dy]
    partners += [(dv, 0, 0, dz) for dv in range(2) for dz in range(nz) if dv or dz]

    load_w = pltpu.make_async_copy(w_hbm, w_in, load_sem.at[1])
    load_w.start()
    load_x = pltpu.make_async_copy(x_hbm, xs, load_sem.at[0])
    load_x.start()
    barrier = pltpu.get_barrier_semaphore()
    for to in partners:
        pl.semaphore_signal(barrier, inc=1, device_id=device(*to), device_id_type=MESH)

    pending = []
    flying = {}

    def send(s, h, name, index, src, dst, to):
        where = places[name] + index
        copy = pltpu.make_async_remote_copy(
            src_ref=src,
            dst_ref=dst,
            send_sem=send_sem.at[s, h, where],
            recv_sem=recv_sem.at[s, h, where],
            device_id=device(*to),
            device_id_type=MESH,
        )
        copy.start()
        flying[s, h, name, index] = copy

    def arrive(s, h, name, index):
        copy = flying.pop((s, h, name, index))
        copy.wait_recv()
        pending.append(copy)

    def drain(keep):
        while len(pending) > keep:
            pending.pop(0).wait_send()

    def gather_z(s, h):
        for slot in reversed(range(1, nz)):
            for p in range(2):
                send(s, h, "gz", slot * 2 + p, wg.at[s, h, p, 0, 0, 0, 0],
                     wg.at[s, h, p, slot // near, 0, 0, slot % near], (0, 0, 0, (nz - offs[slot]) % nz))

    def gather_m(g, s, h):
        for slot in range(g * near, (g + 1) * near):
            for p in range(2):
                if slot:
                    arrive(s, h, "gz", slot * 2 + p)
        for p in range(2):
            src = wg.at[s, h, p, g, 0, 0]
            for e in others:
                send(s, h, "gm", (p * 2 + g) * n + e, src, wg.at[s, h, p, g, 0, e], along_m(p, n - e))
        for p in range(2):
            src = wg.at[s, h, p, g, 0, 0]
            for d in others:
                send(s, h, "gl", ((p * 2 + g) * n + d) * n, src, wg.at[s, h, p, g, d, 0], along_l(p, n - d))

    def gather_l(g, s, h):
        for e in others:
            for p in range(2):
                arrive(s, h, "gm", (p * 2 + g) * n + e)
                src = wg.at[s, h, p, g, 0, e]
                for d in others:
                    send(s, h, "gl", ((p * 2 + g) * n + d) * n + e, src, wg.at[s, h, p, g, d, e], along_l(p, n - d))

    def project(g, s, h):
        for d in [0] + others:
            for p in range(2):
                if d:
                    for e in range(n):
                        arrive(s, h, "gl", ((p * 2 + g) * n + d) * n + e)
                width = n * span
                part = jnp.dot(
                    xp[p, g, :, d * width:(d + 1) * width],
                    wg[s, h, p, g, d].reshape(width, LANES),
                    preferred_element_type=jnp.float32,
                )
                if g or d or p:
                    part += pf[s, h]
                pf[s, h] = part
        if g:
            part = pf[s, h]
            n1[s, h, 0] = jnp.sum(part * part, axis=0, keepdims=True)
            for dx in range(n):
                for dy in range(n):
                    if dx or dy:
                        to = dx * n + dy
                        send(s, h, "n1", to, n1.at[s, h, 0], n1.at[s, h, to], (0, dx, dy, 0))
            send(s, h, "swap", 0, pf.at[s, h], pp.at[s, h], (1, 0, 0, 0))

    def norm_2(s, h):
        for to in range(1, n * n):
            arrive(s, h, "n1", to)
        n2[s, h, 0, 0] = jnp.sum(n1[s, h], axis=0)
        for slot in reversed(range(nz)):
            dz = offs[slot]
            for dv in range(2):
                if dv or dz:
                    send(s, h, "n2", dv * nz + dz, n2.at[s, h, 0, 0], n2.at[s, h, dv, dz], (dv, 0, 0, dz))

    columns = [slice(h * LANES, (h + 1) * LANES) for h in range(blocks)]

    def gradient(s, h):
        arrive(s, h, "swap", 0)
        for dv in range(2):
            for dz in range(nz):
                if dv or dz:
                    arrive(s, h, "n2", dv * nz + dz)
        own_scale = lax.rsqrt(jnp.sum(n2[s, h, 0], axis=0) / total_rows + EPSILON)
        other_scale = lax.rsqrt(jnp.sum(n2[s, h, 1], axis=0) / total_rows + EPSILON)
        own = (pf[s, h] * own_scale).astype(jnp.bfloat16)
        other = (pp[s, h] * other_scale).astype(jnp.bfloat16)
        rr[h] = (own.astype(jnp.float32) - other.astype(jnp.float32)).astype(jnp.bfloat16)
        for g in (1, 0):
            for e in by_m:
                for p in range(2):
                    part = jnp.dot(xt[p, g, :, e].reshape(n * span, rows), rr[h], preferred_element_type=jnp.float32)
                    gs[s, h, p, g, e] = part.astype(jnp.bfloat16).reshape(n, near, PIECE, LANES)
                    for d in others:
                        send(s, h, "r1", ((p * 2 + g) * n + e) * n + d, gs.at[s, h, p, g, e, d],
                             r1.at[s, h, p, g, e, d - 1], along_l(p, d))
        own_w[h] = own_w[h] * own_scale
        if s == ITERS - 1:
            proj_ref[:, columns[h]] = own

    def wide(value):
        return value.astype(jnp.float32)

    def first_sum(s, h, p, g, e):
        for d in others:
            arrive(s, h, "r1", ((p * 2 + g) * n + e) * n + d)
        total = wide(gs[s, h, p, g, e, 0])
        for d in range(n - 1):
            total += wide(r1[s, h, p, g, e, d])
        return total

    def reduce_2(g, s, h):
        for e in others:
            for p in range(2):
                t2[s, h, p, g, e - 1] = first_sum(s, h, p, g, e).astype(jnp.bfloat16)
                send(s, h, "r2", (p * 2 + g) * n + e, t2.at[s, h, p, g, e - 1], r2.at[s, h, p, g, e - 1], along_m(p, e))

    kept = {}

    def reduce_3(g, s, h):
        for p in range(2):
            total = first_sum(s, h, p, g, 0)
            for e in others:
                arrive(s, h, "r2", (p * 2 + g) * n + e)
                total += wide(r2[s, h, p, g, e - 1])
            t3[s, h, g, :, p] = total.astype(jnp.bfloat16)
            if g == 0:
                kept[h, p] = total[0]
        for slot in reversed(range(g * near, (g + 1) * near)):
            if slot:
                send(s, h, "r3", slot, t3.at[s, h, g, slot % near], r3.at[s, h, slot], (0, 0, 0, offs[slot]))

    def update(s, h):
        for slot in reversed(range(1, nz)):
            arrive(s, h, "r3", slot)
        for p in range(2):
            grad = kept.pop((h, p))
            for slot in range(1, nz):
                grad += wide(r3[s, h, slot, p])
            at = slice(p * PIECE, (p + 1) * PIECE)
            new = root * (own_w[h, at] - STEP_RATE * (grad / total_rows))
            if s == ITERS - 1:
                wout_ref[at, columns[h]] = new
            else:
                own_w[h, at] = new
                wg[s + 1, h, p, 0, 0, 0, 0] = new.astype(jnp.bfloat16)
        if s < ITERS - 1:
            gather_z(s + 1, h)

    def choose():
        i = lax.broadcasted_iota(jnp.int32, (strip, strip), 0)
        j = lax.broadcasted_iota(jnp.int32, (strip, strip), 1)
        slot = j // (strip // 2) * near + lax.rem(j // PIECE, near)
        half = lax.rem(j // span, 2)
        wanted = jnp.zeros_like(slot)
        for k in range(nz):
            wanted = jnp.where(slot == k, offs[k], wanted)
        wanted = lax.rem(wanted + z, nz) * 2 * PIECE + lax.rem(j, PIECE)
        for p in range(2):
            for b in range(2):
                hit = jnp.logical_and(i == wanted + p * PIECE, half == b)
                perm[p, b] = jnp.where(hit, 1.0, 0.0).astype(jnp.bfloat16)

    def turn():
        pairs = n // 2

        def one(i, carry):
            l, mp = i // pairs, lax.rem(i, pairs)
            for p in range(2):
                out = None
                for b in range(2):
                    m = mp * 2 + b
                    dx, dy = (l, m) if p == 0 else (m, l)
                    place = (lax.rem(x + dx, n) * n + lax.rem(y + dy, n)) * strip
                    lanes = pl.ds(pl.multiple_of(place, strip), strip)
                    part = jnp.dot(xs[:, lanes], perm[p, b], preferred_element_type=jnp.float32)
                    out = part if out is None else out + part
                out = out.astype(jnp.bfloat16)
                for g in range(2):
                    some = out[:, g * 2 * span:(g + 1) * 2 * span]
                    to = pl.multiple_of(i * 2 * span, 2 * span)
                    xp[p, g, :, pl.ds(to, 2 * span)] = some
                    xt[p, g, l, pl.ds(mp * 2, 2)] = some.T.reshape(2, span, rows)
            return carry

        lax.fori_loop(0, n * pairs, one, 0)

    load_w.wait()
    for h in range(blocks):
        own_w[h] = w_in[:, columns[h]]
        for p in range(2):
            wg[0, h, p, 0, 0, 0, 0] = own_w[h, p * PIECE:(p + 1) * PIECE].astype(jnp.bfloat16)
    pl.semaphore_wait(barrier, len(partners))
    for h in range(blocks):
        gather_z(0, h)
    choose()

    stages = (
        functools.partial(gather_m, 0),
        functools.partial(gather_m, 1),
        functools.partial(gather_l, 0),
        functools.partial(gather_l, 1),
        functools.partial(project, 0),
        functools.partial(project, 1),
        norm_2,
        gradient,
        functools.partial(reduce_2, 1),
        functools.partial(reduce_2, 0),
        functools.partial(reduce_3, 1),
        functools.partial(reduce_3, 0),
        update,
    )
    for s in range(ITERS):
        for i, stage in enumerate(stages):
            if s == 0 and i == 4:
                load_x.wait()
                turn()
            for h in range(blocks):
                drain(200)
                stage(s, h)
    drain(0)


def on_device(dims, views, weights):
    n, nz = dims
    _, rows, feats = views.shape
    _, own_rows, width = weights.shape
    blocks = width // LANES
    _, count = layout(n, nz)
    near = nz // 2
    strip = nz * 2 * PIECE
    half, full, dma = jnp.bfloat16, jnp.float32, pltpu.SemaphoreType.DMA
    lead = (ITERS, blocks)
    tile = (near, PIECE, LANES)
    scratch = [
        pltpu.VMEM((rows, feats), half),
        pltpu.VMEM((own_rows, width), full),
        pltpu.VMEM((2, 2, strip, strip), half),
        pltpu.VMEM((2, 2, rows, feats // 4), half),
        pltpu.VMEM((2, 2, n, n, near * PIECE, rows), half),
        pltpu.VMEM(lead + (2, 2, n, n) + tile, half),
        pltpu.VMEM(lead + (rows, LANES), full),
        pltpu.VMEM(lead + (rows, LANES), full),
        pltpu.VMEM((blocks, rows, LANES), half),
        pltpu.VMEM(lead + (n * n, 1, LANES), full),
        pltpu.VMEM(lead + (2, nz, 1, LANES), full),
        pltpu.VMEM(lead + (2, 2, n, n) + tile, half),
        pltpu.VMEM(lead + (2, 2, n, n - 1) + tile, half),
        pltpu.VMEM(lead + (2, 2, n - 1) + tile, half),
        pltpu.VMEM(lead + (2, 2, n - 1) + tile, half),
        pltpu.VMEM(lead + (2, near, 2, PIECE, LANES), half),
        pltpu.VMEM(lead + (nz, 2, PIECE, LANES), half),
        pltpu.VMEM((blocks, own_rows, LANES), full),
        dma(lead + (count,)),
        dma(lead + (count,)),
        dma((2,)),
    ]
    total_rows = rows * n * n * nz
    vmem = pl.BlockSpec(memory_space=pltpu.VMEM)
    hbm = pl.BlockSpec(memory_space=pl.ANY)
    flops = 4 * ITERS * rows * feats * width
    new, shown = pl.pallas_call(
        functools.partial(kernel, dims, total_rows, math.sqrt(feats)),
        out_shape=(
            jax.ShapeDtypeStruct((own_rows, width), full),
            jax.ShapeDtypeStruct((rows, width), half),
        ),
        in_specs=[hbm, hbm],
        out_specs=(vmem, vmem),
        scratch_shapes=scratch,
        compiler_params=pltpu.CompilerParams(
            collective_id=0, has_side_effects=True, vmem_limit_bytes=56 << 20
        ),
        cost_estimate=pl.CostEstimate(flops=flops, bytes_accessed=2 * rows * feats, transcendentals=0),
        name="cca_steps",
    )(views[0], weights[0])
    return new[None], shown[None]


def solution(mesh):
    dims = (math.isqrt(mesh.shape["row"]), mesh.shape["feat"])
    spec = P("view", ("row", "feat"), None)
    return jax.shard_map(
        functools.partial(on_device, dims),
        mesh=mesh,
        in_specs=(spec, spec),
        out_specs=(spec, spec),
        check_vma=False,
    )
```

time: 2370 us -> 128 us (0.05)
  waiting for transfers between devices: 1620 us -> 0 us
  blocking collectives: 693 us -> 0 us
  Pallas kernels: 0 us -> 122 us
  matrix products: 23.8 us -> 0 us
    reduce_scatter x2 -> x0, waiting for transfers between devices: 1390 us -> none  [on_device(): lax.psum_scatter(lax.dot_general(samples, residue, (((0,), (0,)), ((), ()...]
    psum x2 -> x0, blocking collectives: 693 us -> none  [on_device(): col_sums = lax.psum(squares, ('row', 'feat'))]
    all_gather x2 -> x0, waiting for transfers between devices: 229 us -> none  [on_device(): whole_dirs = lax.all_gather(halved, ('row', 'feat'), axis=0, tiled=True)]
    pallas_call x0 -> x1, Pallas kernels: none -> 122 us  [on_device(): pl.pallas_call(functools.partial(kernel, dims, total_rows, math.sqrt(feat...]
    dot_general x4 -> x0, matrix products: 23.8 us -> none  [the longest x2 13.2 us: on_device(): lax.dot_general(samples, residue, (((0,), (0,)), ((), ())), preferred_ele...]
  transfers between devices with their start and end apart: 6 -> 0, of which waited for: 6 -> 0; matrix products, arithmetic and copies ran while one was open for 0% -> 0% of each run, Pallas kernels for 0% -> 0%
where the time goes in v1:
time: 128 us; the launch traced here: 126 us
  Pallas kernels  122 us (95%)
  local copies, waits for them, and re-layouts  3.14 us (2%)
    pallas_call x1, Pallas kernels, on_device(): pl.pallas_call(functools.partial(kernel, dims, total_rows, math.sqrt(feat...  122 us
    unnamed x2, local copies, waits for them, and re-layouts  3.14 us

profile of v1, /device:TPU:0, one launch (start us, length us, event | category | flops | bytes accessed | tf_op | source)
XLA Modules:
  0.0 126.2 jit_solution(5197276886298689694)
XLA Ops:
  0.6 122.4 %cca_steps.1 = (f32[32,256]{1,0:T(8,128)}, bf16[768,256]{1,0:T(8,128)(2,1)}) custom-call(bf16[768,4096]{1,0:T(8,128)(2,1)} %bitcast.6, f32[32,256]{1,0:T(8,128)} %bitcast.7), custom_call_target="tpu_custom_call" | custom-call | flops 6442450944 | bytes 6291456 | tf_op jit(solution)/shard_map/cca_steps/pallas_call | solution.py:358
  123.1 1.4 %copy.6 = f32[1,32,256]{2,1,0:T(8,128)} copy(f32[1,32,256]{2,1,0:T(8,128)} %bitcast.5) | data formatting | bytes 65536
  124.4 1.8 %copy.7 = bf16[1,768,256]{2,1,0:T(8,128)(2,1)} copy(bf16[1,768,256]{2,1,0:T(8,128)(2,1)} %bitcast.4) | data formatting | bytes 786432

commit v2 on v1

v2 whole, which is shorter than its diff:
```python
import functools
import math

import jax
import jax.numpy as jnp
from jax import lax
from jax.experimental import pallas as pl
from jax.experimental.pallas import tpu as pltpu
from jax.sharding import PartitionSpec as P

ITERS = 2
EPSILON = 1e-06
STEP_RATE = 0.5
TURN_AT = 4
WIDE = 256
HALF = 128
PIECE = 16
MESH = pl.DeviceIdType.MESH
ODD_0, EVEN_0, EVEN_1 = range(3)


def arrivals(n):
    sizes = {
        "gz": 2,
        "gm": 2 * n,
        "gl": 2 * n,
        "zf": n,
        "n1": 1,
        "n2": ITERS,
        "swap": ITERS,
        "rz": n,
        "r1": 3 * n,
        "r2": 3,
        "r3": 2,
    }
    start, places = 0, {}
    for name, count in sizes.items():
        places[name] = start
        start += count
    return places, start


DEPARTURES = ("gz0", "gz1", "gm0", "gm1", "gl0", "gl1", "zf", "n1", "n2", "swap", "rz", "r1", "r2", "r30", "r31")


def slots(nz):
    reach = nz // 4
    even = [2 * i for i in reversed(range(reach))] + [-2 * i for i in range(1, reach)] + [2 * reach]
    odd = [2 * i + 1 for i in reversed(range(reach))] + [-2 * i - 1 for i in range(reach)]
    return [d % nz for d in even + odd], reach


def kernel(dims, total_rows, root, x_hbm, w_hbm, wout_ref, proj_ref, *scratch):
    n, nz = dims
    (xs, own_w, perm, xp, xt, wg, pf, pp, rr, n1, n2, gs, go, rz, r1, t2, r2, t3, t3o, r3, r3o,
     send_sem, recv_sem, load_sem) = scratch
    rows, feats = xs.shape
    near = nz // 2
    offs, reach = slots(nz)
    mine = reach - 1
    first, second = pl.ds(0, HALF), pl.ds(HALF, HALF)
    up, down = pl.ds(0, reach), pl.ds(mine, reach)
    odd_up, odd_down = pl.ds(0, reach), pl.ds(reach, reach)
    places, _ = arrivals(n)
    strip = nz * 2 * PIECE
    span = near * PIECE
    others = sorted(range(1, n), key=lambda d: (min(d, n - d), d))
    by_m = others + [0]

    v = lax.axis_index("view")
    r = lax.axis_index("row")
    z = lax.axis_index("feat")
    x, y = r // n, lax.rem(r, n)

    def ahead(i, d, size):
        return lax.rem(i + d, size) if d else i

    def device(dv, dx, dy, dz):
        return (ahead(v, dv, 2), ahead(x, dx, n) * n + ahead(y, dy, n), ahead(z, dz, nz))

    def along_l(p, d):
        return (0, d, 0, 0) if p == 0 else (0, 0, d, 0)

    def along_m(p, d):
        return (0, 0, d, 0) if p == 0 else (0, d, 0, 0)

    partners = [(0, dx, dy, 0) for dx in range(n) for dy in range(n) if dx or dy]
    partners += [(dv, 0, 0, dz) for dv in range(2) for dz in range(nz) if dv or dz]

    barrier = pltpu.get_barrier_semaphore()
    for to in partners:
        pl.semaphore_signal(barrier, inc=1, device_id=device(*to), device_id_type=MESH)
    load_w = pltpu.make_async_copy(w_hbm, own_w, load_sem.at[1])
    load_w.start()
    load_x = pltpu.make_async_copy(x_hbm, xs, load_sem.at[0])
    load_x.start()

    def sent(s, name):
        g = int(name[2:]) if name[:2] in ("gz", "gm", "gl", "r3") else 0
        rest = pl.ds(1, n - 1)
        wide_or_half = wg.at[s, :, g] if g == 0 else wg.at[s, :, g, :, :, :, :, first]
        return {
            "gz": wg.at[s, :, 0, 0, 0, pl.ds(0, near - 1)] if g == 0 else wg.at[s, :, 1, 0, 0, :, :, first],
            "gm": wide_or_half.at[:, 0, rest],
            "gl": wide_or_half.at[:, rest],
            "zf": wg.at[s, :, 1, :, :, :, :, second],
            "n1": n1.at[s, pl.ds(1, n * n - 1)],
            "n2": n2.at[s, pl.ds(1, 2 * nz - 1)],
            "sw": pp.at[s],
            "rz": rz.at[s],
            "r1": r1.at[s],
            "r2": r2.at[s],
            "r3": r3.at[s, pl.ds(0, near - 1)] if g == 0 else r3o.at[s],
        }[name[:2]]

    def copy_of(src, dst, out, name, index, to):
        return pltpu.make_async_remote_copy(
            src_ref=src,
            dst_ref=dst,
            send_sem=send_sem.at[DEPARTURES.index(out)],
            recv_sem=recv_sem.at[places[name] + index],
            device_id=device(*to),
            device_id_type=MESH,
        )

    busy = {}

    def leave(out):
        if out in busy:
            whole = sent(busy.pop(out), out)
            copy_of(whole, whole, out, "gz", 0, (1, 0, 0, 0)).wait_send()

    def send(s, out, index, src, dst, to):
        if busy.get(out, s) != s:
            leave(out)
        busy[out] = s
        name = out if out in places else out[:2]
        copy_of(src, dst, out, name, index, to).start()

    def arrive(name, index, whole):
        copy_of(whole, whole, "gz0", name, index, (1, 0, 0, 0)).wait_recv()

    def part_of(s, p, g, d, e):
        return wg.at[s, p, g, d, e] if g == 0 else wg.at[s, p, g, d, e, :, :, first]

    def gather_z(s):
        for slot in sorted(range(nz), key=lambda k: (k // near, -min(offs[k], nz - offs[k]))):
            if slot == mine:
                continue
            g = slot // near
            for p in range(2):
                src = wg.at[s, p, 0, 0, 0, mine]
                dst = wg.at[s, p, g, 0, 0, slot % near]
                if g:
                    src, dst = src.at[:, first], dst.at[:, first]
                send(s, f"gz{g}", g, src, dst, (0, 0, 0, nz - offs[slot]))

    def forward(s, d):
        for p in range(2):
            even, odd = wg.at[s, p, 0, d], wg.at[s, p, 1, d]
            send(s, "zf", d, even.at[:, up, :, second], odd.at[:, odd_up, :, second], (0, 0, 0, nz - 1))
            send(s, "zf", d, even.at[:, down, :, second], odd.at[:, odd_down, :, second], (0, 0, 0, 1))

    def gather_m(g, s):
        arrive("gz", g, sent(s, f"gz{g}"))
        for p in range(2):
            src = part_of(s, p, g, 0, 0)
            for e in others:
                send(s, f"gm{g}", g * n + e, src, part_of(s, p, g, 0, e), along_m(p, n - e))
        for p in range(2):
            src = part_of(s, p, g, 0, 0)
            for d in others:
                send(s, f"gl{g}", g * n + d, src, part_of(s, p, g, d, 0), along_l(p, n - d))

    def both(s, g):
        return wg.at[s, :, 0] if g == 0 else wg.at[s, :, 1, :, :, :, :, first]

    def gather_l(g, s):
        for e in others:
            arrive("gm", g * n + e, both(s, g).at[:, 0, e])
            for p in range(2):
                src = part_of(s, p, g, 0, e)
                for d in others:
                    send(s, f"gl{g}", g * n + d, src, part_of(s, p, g, d, e), along_l(p, n - d))
        if g == 0:
            forward(s, 0)

    def gather_far(s):
        for d in others:
            arrive("gl", d, both(s, 0).at[:, d])
            forward(s, d)

    def project(g, s):
        for d in [0] + others:
            if g:
                if d:
                    arrive("gl", n + d, both(s, 1).at[:, d])
                arrive("zf", d, wg.at[s, :, 1, d, :, :, :, second])
            for p in range(2):
                width = n * span
                part = jnp.dot(
                    xp[p, g, :, d * width:(d + 1) * width],
                    wg[s, p, g, d].reshape(width, WIDE),
                    preferred_element_type=jnp.float32,
                )
                if g or d or p:
                    part += pf[s]
                pf[s] = part

    def norm_1(s):
        part = pf[s]
        n1[s, 0] = jnp.sum(part * part, axis=0, keepdims=True)
        for dx in range(n):
            for dy in range(n):
                if dx or dy:
                    send(s, "n1", 0, n1.at[s, 0], n1.at[s, dx * n + dy], (0, dx, dy, 0))
        send(s, "swap", s, pf.at[s], pp.at[s], (1, 0, 0, 0))

    def norm_2(s):
        arrive("n1", 0, sent(s, "n1"))
        n2[s, 0] = jnp.sum(n1[s], axis=0)
        for dz in sorted(range(nz), key=lambda d: -min(d, nz - d)):
            for dv in range(2):
                if dv or dz:
                    send(s, "n2", s, n2.at[s, 0], n2.at[s, dv * nz + dz], (dv, 0, 0, dz))

    def wide(value):
        return value.astype(jnp.float32)

    def spread(s, k, p, e):
        for d in others:
            send(s, "r1", k * n + e, gs.at[s, k, p, e, d], r1.at[s, k, e, p, d - 1], along_l(p, d))

    def gradient(s):
        arrive("swap", s, pp.at[s])
        arrive("n2", s, sent(s, "n2"))
        own_scale = lax.rsqrt(jnp.sum(n2[s, :nz], axis=0) / total_rows + EPSILON)
        other_scale = lax.rsqrt(jnp.sum(n2[s, nz:], axis=0) / total_rows + EPSILON)
        own = (pf[s] * own_scale).astype(jnp.bfloat16)
        other = (pp[s] * other_scale).astype(jnp.bfloat16)
        rr[...] = (wide(own) - wide(other)).astype(jnp.bfloat16)
        for g in (1, 0):
            for e in by_m:
                for p in range(2):
                    part = jnp.dot(xt[p, g, :, e].reshape(n * span, rows), rr[...], preferred_element_type=jnp.float32)
                    part = part.astype(jnp.bfloat16).reshape(n, near, PIECE, WIDE)
                    gs[s, EVEN_0 if g == 0 else ODD_0, p, e] = part[..., :HALF]
                    if g == 0:
                        gs[s, EVEN_1, p, e] = part[..., HALF:]
                        spread(s, EVEN_0, p, e)
                    else:
                        go[s, p, e] = part[..., HALF:]
                        send(s, "rz", e, go.at[s, p, e, :, odd_up], rz.at[s, e, p, 0], (0, 0, 0, 1))
                        send(s, "rz", e, go.at[s, p, e, :, odd_down], rz.at[s, e, p, 1], (0, 0, 0, nz - 1))
                        spread(s, ODD_0, p, e)
        own_w[...] = own_w[...] * own_scale
        if s == ITERS - 1:
            proj_ref[...] = own

    def reduce_z(s):
        for e in by_m:
            arrive("rz", e, rz.at[s, e])
            for p in range(2):
                for k in range(near):
                    total = wide(gs[s, EVEN_1, p, e, :, k])
                    if k < reach:
                        total += wide(rz[s, e, p, 0, :, k])
                    if mine <= k < mine + reach:
                        total += wide(rz[s, e, p, 1, :, k - mine])
                    if k < mine + reach:
                        gs[s, EVEN_1, p, e, :, k] = total.astype(jnp.bfloat16)
                spread(s, EVEN_1, p, e)

    def first_sum(s, k, p, e):
        if p == 0:
            arrive("r1", k * n + e, r1.at[s, k, e])
        total = wide(gs[s, k, p, e, 0])
        for d in range(n - 1):
            total += wide(r1[s, k, e, p, d])
        return total

    def reduce_2(k, s):
        for e in others:
            for p in range(2):
                t2[s, k, p, e - 1] = first_sum(s, k, p, e).astype(jnp.bfloat16)
                send(s, "r2", k, t2.at[s, k, p, e - 1], r2.at[s, k, p, e - 1], along_m(p, e))

    kept = {}

    def second_sum(s, k, p):
        total = first_sum(s, k, p, 0)
        if p == 0:
            arrive("r2", k, r2.at[s, k])
        for e in others:
            total += wide(r2[s, k, p, e - 1])
        if k != ODD_0:
            kept[k, p] = total[mine]
        return total.astype(jnp.bfloat16)

    def reduce_3(g, s):
        for p in range(2):
            if g:
                t3o[s, :, p] = second_sum(s, ODD_0, p)
            else:
                t3[s, :, p, :, :HALF] = second_sum(s, EVEN_0, p)
                t3[s, :, p, :, HALF:] = second_sum(s, EVEN_1, p)
        for slot in sorted(range(g * near, (g + 1) * near), key=lambda k: -min(offs[k], nz - offs[k])):
            k = slot % near
            if g:
                send(s, "r31", 1, t3o.at[s, k], r3o.at[s, k], (0, 0, 0, offs[slot]))
            elif slot != mine:
                send(s, "r30", 0, t3.at[s, k], r3.at[s, k - (k > mine)], (0, 0, 0, offs[slot]))

    def update(s):
        arrive("r3", 1, r3o.at[s])
        arrive("r3", 0, sent(s, "r30"))
        for p in range(2):
            at = slice(p * PIECE, (p + 1) * PIECE)
            for c, k in enumerate((EVEN_0, EVEN_1)):
                columns = slice(c * HALF, (c + 1) * HALF)
                grad = kept.pop((k, p))
                for slot in range(near):
                    if slot != mine:
                        grad += wide(r3[s, slot - (slot > mine), p, :, columns])
                    if c == 0:
                        grad += wide(r3o[s, slot, p])
                new = root * (own_w[at, columns] - STEP_RATE * (grad / total_rows))
                if s == ITERS - 1:
                    wout_ref[at, columns] = new
                else:
                    own_w[at, columns] = new
                    wg[s + 1, p, 0, 0, 0, mine, :, columns] = new.astype(jnp.bfloat16)
        if s < ITERS - 1:
            gather_z(s + 1)

    def choose():
        i = lax.broadcasted_iota(jnp.int32, (strip, strip), 0)
        j = lax.broadcasted_iota(jnp.int32, (strip, strip), 1)
        slot = j // (strip // 2) * near + lax.rem(j // PIECE, near)
        half = lax.rem(j // span, 2)
        wanted = jnp.zeros_like(slot)
        for k in range(nz):
            wanted = jnp.where(slot == k, offs[k], wanted)
        wanted = lax.rem(wanted + z, nz) * 2 * PIECE + lax.rem(j, PIECE)
        for p in range(2):
            for b in range(2):
                hit = jnp.logical_and(i == wanted + p * PIECE, half == b)
                perm[p, b] = jnp.where(hit, 1.0, 0.0).astype(jnp.bfloat16)

    def turn():
        pairs = n // 2

        def one(i, carry):
            l, mp = i // pairs, lax.rem(i, pairs)
            for p in range(2):
                out = None
                for b in range(2):
                    m = mp * 2 + b
                    dx, dy = (l, m) if p == 0 else (m, l)
                    place = (lax.rem(x + dx, n) * n + lax.rem(y + dy, n)) * strip
                    lanes = pl.ds(pl.multiple_of(place, strip), strip)
                    part = jnp.dot(xs[:, lanes], perm[p, b], preferred_element_type=jnp.float32)
                    out = part if out is None else out + part
                out = out.astype(jnp.bfloat16)
                for g in range(2):
                    some = out[:, g * 2 * span:(g + 1) * 2 * span]
                    to = pl.multiple_of(i * 2 * span, 2 * span)
                    xp[p, g, :, pl.ds(to, 2 * span)] = some
                    xt[p, g, l, pl.ds(mp * 2, 2)] = some.T.reshape(2, span, rows)
            return carry

        lax.fori_loop(0, n * pairs, one, 0)

    load_w.wait()
    for p in range(2):
        wg[0, p, 0, 0, 0, mine] = own_w[p * PIECE:(p + 1) * PIECE, :].astype(jnp.bfloat16)
    pl.semaphore_wait(barrier, len(partners))
    gather_z(0)
    choose()

    stages = (
        functools.partial(gather_m, 0),
        functools.partial(gather_m, 1),
        functools.partial(gather_l, 0),
        functools.partial(gather_l, 1),
        gather_far,
        functools.partial(project, 0),
        functools.partial(project, 1),
        norm_1,
        norm_2,
        gradient,
        reduce_z,
        functools.partial(reduce_2, ODD_0),
        functools.partial(reduce_2, EVEN_0),
        functools.partial(reduce_2, EVEN_1),
        functools.partial(reduce_3, 1),
        functools.partial(reduce_3, 0),
        update,
    )
    for s in range(ITERS):
        for i, stage in enumerate(stages):
            if s == 0 and i == TURN_AT:
                load_x.wait()
                turn()
            stage(s)
    for out in DEPARTURES:
        leave(out)


def on_device(dims, views, weights):
    n, nz = dims
    _, rows, feats = views.shape
    _, own_rows, width = weights.shape
    _, count = arrivals(n)
    near, reach = nz // 2, nz // 4
    strip = nz * 2 * PIECE
    half, full, dma = jnp.bfloat16, jnp.float32, pltpu.SemaphoreType.DMA
    lead = (ITERS,)
    tile = (near, PIECE, HALF)
    scratch = [
        pltpu.VMEM((rows, feats), half),
        pltpu.VMEM((own_rows, width), full),
        pltpu.VMEM((2, 2, strip, strip), half),
        pltpu.VMEM((2, 2, rows, feats // 4), half),
        pltpu.VMEM((2, 2, n, n, near * PIECE, rows), half),
        pltpu.VMEM(lead + (2, 2, n, n, near, PIECE, width), half),
        pltpu.VMEM(lead + (rows, width), full),
        pltpu.VMEM(lead + (rows, width), full),
        pltpu.VMEM((rows, width), half),
        pltpu.VMEM(lead + (n * n, 1, width), full),
        pltpu.VMEM(lead + (2 * nz, 1, width), full),
        pltpu.VMEM(lead + (3, 2, n, n) + tile, half),
        pltpu.VMEM(lead + (2, n, n) + tile, half),
        pltpu.VMEM(lead + (n, 2, 2, n, reach, PIECE, HALF), half),
        pltpu.VMEM(lead + (3, n, 2, n - 1) + tile, half),
        pltpu.VMEM(lead + (3, 2, n - 1) + tile, half),
        pltpu.VMEM(lead + (3, 2, n - 1) + tile, half),
        pltpu.VMEM(lead + (near, 2, PIECE, width), half),
        pltpu.VMEM(lead + (near, 2, PIECE, HALF), half),
        pltpu.VMEM(lead + (near, 2, PIECE, width), half),
        pltpu.VMEM(lead + (near, 2, PIECE, HALF), half),
        dma((len(DEPARTURES),)),
        dma((count,)),
        dma((2,)),
    ]
    total_rows = rows * n * n * nz
    vmem = pl.BlockSpec(memory_space=pltpu.VMEM)
    hbm = pl.BlockSpec(memory_space=pl.ANY)
    flops = 4 * ITERS * rows * feats * width
    new, shown = pl.pallas_call(
        functools.partial(kernel, dims, total_rows, math.sqrt(feats)),
        out_shape=(
            jax.ShapeDtypeStruct((own_rows, width), full),
            jax.ShapeDtypeStruct((rows, width), half),
        ),
        in_specs=[hbm, hbm],
        out_specs=(vmem, vmem),
        scratch_shapes=scratch,
        compiler_params=pltpu.CompilerParams(
            collective_id=0, has_side_effects=True, vmem_limit_bytes=56 << 20
        ),
        cost_estimate=pl.CostEstimate(flops=flops, bytes_accessed=2 * rows * feats, transcendentals=0),
        name="cca_steps",
    )(views[0], weights[0])
    return new[None], shown[None]


def solution(mesh):
    dims = (math.isqrt(mesh.shape["row"]), mesh.shape["feat"])
    spec = P("view", ("row", "feat"), None)
    return jax.shard_map(
        functools.partial(on_device, dims),
        mesh=mesh,
        in_specs=(spec, spec),
        out_specs=(spec, spec),
        check_vma=False,
    )
```

time: 128 us -> 117 us (0.914)
  Pallas kernels: 122 us -> 112 us
    pallas_call x1, Pallas kernels: 122 us -> 112 us  [on_device(): pl.pallas_call(functools.partial(kernel, dims, total_rows, math.sqrt(feat...]
where the time goes in v2:
time: 117 us; the launch traced here: 116 us
  Pallas kernels  112 us (96%)
  local copies, waits for them, and re-layouts  3.14 us (3%)
    pallas_call x1, Pallas kernels, on_device(): pl.pallas_call(functools.partial(kernel, dims, total_rows, math.sqrt(feat...  112 us
    unnamed x2, local copies, waits for them, and re-layouts  3.14 us

profile of v2, /device:TPU:0, one launch (start us, length us, event | category | flops | bytes accessed | tf_op | source)
XLA Modules:
  0.0 115.9 jit_solution(12225106446037512139)
XLA Ops:
  0.6 112.1 %cca_steps.1 = (f32[32,256]{1,0:T(8,128)}, bf16[768,256]{1,0:T(8,128)(2,1)}) custom-call(bf16[768,4096]{1,0:T(8,128)(2,1)} %bitcast.6, f32[32,256]{1,0:T(8,128)} %bitcast.7), custom_call_target="tpu_custom_call" | custom-call | flops 6442450944 | bytes 6291456 | tf_op jit(solution)/shard_map/cca_steps/pallas_call | solution.py:450
  112.8 1.4 %copy.6 = f32[1,32,256]{2,1,0:T(8,128)} copy(f32[1,32,256]{2,1,0:T(8,128)} %bitcast.5) | data formatting | bytes 65536
  114.2 1.8 %copy.7 = bf16[1,768,256]{2,1,0:T(8,128)(2,1)} copy(bf16[1,768,256]{2,1,0:T(8,128)(2,1)} %bitcast.4) | data formatting | bytes 786432

commit v3 on v2

--- a/solution.py
+++ b/solution.py
@@ -11,26 +11,25 @@
 ITERS = 2
 EPSILON = 1e-06
 STEP_RATE = 0.5
-TURN_AT = 4
 WIDE = 256
 HALF = 128
 PIECE = 16
 MESH = pl.DeviceIdType.MESH
-ODD_0, EVEN_0, EVEN_1 = range(3)
+ODD_0, EVEN_0, EVEN_1, AHEAD = range(4)
 
 
 def arrivals(n):
     sizes = {
-        "gz": 2,
-        "gm": 2 * n,
+        "gz": 3,
+        "gm": 4 * n,
         "gl": 2 * n,
         "zf": n,
         "n1": 1,
         "n2": ITERS,
         "swap": ITERS,
         "rz": n,
-        "r1": 3 * n,
-        "r2": 3,
+        "r1": 4 * n,
+        "r2": 4,
         "r3": 2,
     }
     start, places = 0, {}
@@ -58,6 +57,8 @@
     near = nz // 2
     offs, reach = slots(nz)
     mine = reach - 1
+    groups = [[mine], [k for k in range(near - 1) if k != mine], [near - 1]]
+    odd_group = len(groups)
     first, second = pl.ds(0, HALF), pl.ds(HALF, HALF)
     up, down = pl.ds(0, reach), pl.ds(mine, reach)
     odd_up, odd_down = pl.ds(0, reach), pl.ds(reach, reach)
@@ -65,7 +66,9 @@
     strip = nz * 2 * PIECE
     span = near * PIECE
     others = sorted(range(1, n), key=lambda d: (min(d, n - d), d))
-    by_m = others + [0]
+    far_first = sorted(others, key=lambda d: -min(d, n - d))
+    by_m = far_first + [0]
+    extent = {ODD_0: (ODD_0, 0, near), EVEN_0: (EVEN_0, 0, near), EVEN_1: (EVEN_1, 0, near - 1), AHEAD: (EVEN_1, near - 1, near)}
 
     v = lax.axis_index("view")
     r = lax.axis_index("row")
@@ -143,17 +146,21 @@
     def part_of(s, p, g, d, e):
         return wg.at[s, p, g, d, e] if g == 0 else wg.at[s, p, g, d, e, :, :, first]
 
+    def rows_of(s, p, d, e, group):
+        if group == odd_group:
+            return [part_of(s, p, 1, d, e)]
+        return [wg.at[s, p, 0, d, e, k] for k in groups[group]]
+
     def gather_z(s):
-        for slot in sorted(range(nz), key=lambda k: (k // near, -min(offs[k], nz - offs[k]))):
-            if slot == mine:
-                continue
-            g = slot // near
-            for p in range(2):
-                src = wg.at[s, p, 0, 0, 0, mine]
-                dst = wg.at[s, p, g, 0, 0, slot % near]
-                if g:
-                    src, dst = src.at[:, first], dst.at[:, first]
-                send(s, f"gz{g}", g, src, dst, (0, 0, 0, nz - offs[slot]))
+        for group in (1, 2, odd_group):
+            g = group // odd_group
+            for k in range(near) if g else groups[group]:
+                for p in range(2):
+                    src = wg.at[s, p, 0, 0, 0, mine]
+                    dst = wg.at[s, p, g, 0, 0, k]
+                    if g:
+                        src, dst = src.at[:, first], dst.at[:, first]
+                    send(s, f"gz{g}", group - 1, src, dst, (0, 0, 0, nz - offs[g * near + k]))
 
     def forward(s, d):
         for p in range(2):
@@ -161,28 +168,34 @@
             send(s, "zf", d, even.at[:, up, :, second], odd.at[:, odd_up, :, second], (0, 0, 0, nz - 1))
             send(s, "zf", d, even.at[:, down, :, second], odd.at[:, odd_down, :, second], (0, 0, 0, 1))
 
-    def gather_m(g, s):
-        arrive("gz", g, sent(s, f"gz{g}"))
-        for p in range(2):
-            src = part_of(s, p, g, 0, 0)
-            for e in others:
-                send(s, f"gm{g}", g * n + e, src, part_of(s, p, g, 0, e), along_m(p, n - e))
-        for p in range(2):
-            src = part_of(s, p, g, 0, 0)
-            for d in others:
-                send(s, f"gl{g}", g * n + d, src, part_of(s, p, g, d, 0), along_l(p, n - d))
-
     def both(s, g):
         return wg.at[s, :, 0] if g == 0 else wg.at[s, :, 1, :, :, :, :, first]
 
-    def gather_l(g, s):
+    def gather_m(group, s):
+        g = group // odd_group
+        if g:
+            arrive("gz", group - 1, sent(s, "gz1"))
+        elif group:
+            arrive("gz", group - 1, wg.at[s, :, 0, 0, 0, pl.ds(0, len(groups[group]))])
+        for p in range(2):
+            for e in far_first:
+                for src, dst in zip(rows_of(s, p, 0, 0, group), rows_of(s, p, 0, e, group)):
+                    send(s, f"gm{g}", group * n + e, src, dst, along_m(p, n - e))
+        for p in range(2):
+            for d in far_first:
+                for src, dst in zip(rows_of(s, p, 0, 0, group), rows_of(s, p, d, 0, group)):
+                    send(s, f"gl{g}", g * n + d, src, dst, along_l(p, n - d))
+
+    def gather_l(group, s):
+        g = group // odd_group
         for e in others:
-            arrive("gm", g * n + e, both(s, g).at[:, 0, e])
+            here = both(s, g).at[:, 0, e]
+            arrive("gm", group * n + e, here if g else here.at[:, pl.ds(0, len(groups[group]))])
             for p in range(2):
-                src = part_of(s, p, g, 0, e)
-                for d in others:
-                    send(s, f"gl{g}", g * n + d, src, part_of(s, p, g, d, e), along_l(p, n - d))
-        if g == 0:
+                for d in far_first:
+                    for src, dst in zip(rows_of(s, p, 0, e, group), rows_of(s, p, d, e, group)):
+                        send(s, f"gl{g}", g * n + d, src, dst, along_l(p, n - d))
+        if group == odd_group - 1:
             forward(s, 0)
 
     def gather_far(s):
@@ -210,10 +223,9 @@
     def norm_1(s):
         part = pf[s]
         n1[s, 0] = jnp.sum(part * part, axis=0, keepdims=True)
-        for dx in range(n):
-            for dy in range(n):
-                if dx or dy:
-                    send(s, "n1", 0, n1.at[s, 0], n1.at[s, dx * n + dy], (0, dx, dy, 0))
+        far = lambda d: -min(d // n, n - d // n) - min(d % n, n - d % n)
+        for to in sorted(range(1, n * n), key=far):
+            send(s, "n1", 0, n1.at[s, 0], n1.at[s, to], (0, to // n, to % n, 0))
         send(s, "swap", s, pf.at[s], pp.at[s], (1, 0, 0, 0))
 
     def norm_2(s):
@@ -227,9 +239,14 @@
     def wide(value):
         return value.astype(jnp.float32)
 
-    def spread(s, k, p, e):
-        for d in others:
-            send(s, "r1", k * n + e, gs.at[s, k, p, e, d], r1.at[s, k, e, p, d - 1], along_l(p, d))
+    def within(i):
+        k, low, high = extent[i]
+        return k, pl.ds(low, high - low)
+
+    def spread(s, i, p, e):
+        k, part = within(i)
+        for d in far_first:
+            send(s, "r1", i * n + e, gs.at[s, k, p, e, d, part], r1.at[s, k, e, p, d - 1, part], along_l(p, d))
 
     def gradient(s):
         arrive("swap", s, pp.at[s])
@@ -248,6 +265,7 @@
                     if g == 0:
                         gs[s, EVEN_1, p, e] = part[..., HALF:]
                         spread(s, EVEN_0, p, e)
+                        spread(s, AHEAD, p, e)
                     else:
                         go[s, p, e] = part[..., HALF:]
                         send(s, "rz", e, go.at[s, p, e, :, odd_up], rz.at[s, e, p, 0], (0, 0, 0, 1))
@@ -257,59 +275,69 @@
         if s == ITERS - 1:
             proj_ref[...] = own
 
-    def reduce_z(s):
-        for e in by_m:
+    def reduce_z(some, s):
+        for e in some:
             arrive("rz", e, rz.at[s, e])
             for p in range(2):
-                for k in range(near):
+                for k in range(near - 1):
                     total = wide(gs[s, EVEN_1, p, e, :, k])
                     if k < reach:
                         total += wide(rz[s, e, p, 0, :, k])
-                    if mine <= k < mine + reach:
+                    if k >= mine:
                         total += wide(rz[s, e, p, 1, :, k - mine])
-                    if k < mine + reach:
-                        gs[s, EVEN_1, p, e, :, k] = total.astype(jnp.bfloat16)
+                    gs[s, EVEN_1, p, e, :, k] = total.astype(jnp.bfloat16)
                 spread(s, EVEN_1, p, e)
 
-    def first_sum(s, k, p, e):
+    def first_sum(s, i, p, e):
+        k, part = within(i)
         if p == 0:
-            arrive("r1", k * n + e, r1.at[s, k, e])
-        total = wide(gs[s, k, p, e, 0])
+            arrive("r1", i * n + e, r1.at[s, k, e, :, :, part])
+        total = wide(gs[s, k, p, e, 0, part])
         for d in range(n - 1):
-            total += wide(r1[s, k, e, p, d])
+            total += wide(r1[s, k, e, p, d, part])
         return total
 
-    def reduce_2(k, s):
+    def reduce_2(i, s):
+        k, part = within(i)
+        for e in far_first:
+            for p in range(2):
+                t2[s, k, p, e - 1, part] = first_sum(s, i, p, e).astype(jnp.bfloat16)
+                send(s, "r2", i, t2.at[s, k, p, e - 1, part], r2.at[s, k, p, e - 1, part], along_m(p, e))
+
+    kept = {}
+
+    def second_sum(s, i, p):
+        k, part = within(i)
+        total = first_sum(s, i, p, 0)
+        if p == 0:
+            arrive("r2", i, r2.at[s, k, :, :, part])
         for e in others:
-            for p in range(2):
-                t2[s, k, p, e - 1] = first_sum(s, k, p, e).astype(jnp.bfloat16)
-                send(s, "r2", k, t2.at[s, k, p, e - 1], r2.at[s, k, p, e - 1], along_m(p, e))
-
-    kept = {}
-
-    def second_sum(s, k, p):
-        total = first_sum(s, k, p, 0)
-        if p == 0:
-            arrive("r2", k, r2.at[s, k])
-        for e in others:
-            total += wide(r2[s, k, p, e - 1])
-        if k != ODD_0:
-            kept[k, p] = total[mine]
+            total += wide(r2[s, k, p, e - 1, part])
+        if i in (EVEN_0, EVEN_1):
+            kept[i, p] = total[mine]
         return total.astype(jnp.bfloat16)
 
-    def reduce_3(g, s):
-        for p in range(2):
-            if g:
-                t3o[s, :, p] = second_sum(s, ODD_0, p)
-            else:
-                t3[s, :, p, :, :HALF] = second_sum(s, EVEN_0, p)
-                t3[s, :, p, :, HALF:] = second_sum(s, EVEN_1, p)
-        for slot in sorted(range(g * near, (g + 1) * near), key=lambda k: -min(offs[k], nz - offs[k])):
-            k = slot % near
-            if g:
-                send(s, "r31", 1, t3o.at[s, k], r3o.at[s, k], (0, 0, 0, offs[slot]))
-            elif slot != mine:
-                send(s, "r30", 0, t3.at[s, k], r3.at[s, k - (k > mine)], (0, 0, 0, offs[slot]))
+    def reduce_3_odd(s):
+        for p in range(2):
+            t3o[s, :, p] = second_sum(s, ODD_0, p)
+        for k in sorted(range(near), key=lambda k: -min(offs[near + k], nz - offs[near + k])):
+            send(s, "r31", 1, t3o.at[s, k], r3o.at[s, k], (0, 0, 0, offs[near + k]))
+
+    def send_even(s, k):
+        send(s, "r30", 0, t3.at[s, k], r3.at[s, k - (k > mine)], (0, 0, 0, offs[k]))
+
+    def reduce_3_ahead(s):
+        for p in range(2):
+            t3[s, :, p, :, :HALF] = second_sum(s, EVEN_0, p)
+            t3[s, near - 1:, p, :, HALF:] = second_sum(s, AHEAD, p)
+        send_even(s, near - 1)
+
+    def reduce_3_even(s):
+        for p in range(2):
+            t3[s, :near - 1, p, :, HALF:] = second_sum(s, EVEN_1, p)
+        for k in range(near - 1):
+            if k != mine:
+                send_even(s, k)
 
     def update(s):
         arrive("r3", 1, r3o.at[s])
@@ -347,7 +375,7 @@
                 hit = jnp.logical_and(i == wanted + p * PIECE, half == b)
                 perm[p, b] = jnp.where(hit, 1.0, 0.0).astype(jnp.bfloat16)
 
-    def turn():
+    def turn(begin, end):
         pairs = n // 2
 
         def one(i, carry):
@@ -369,40 +397,49 @@
                     xt[p, g, l, pl.ds(mp * 2, 2)] = some.T.reshape(2, span, rows)
             return carry
 
-        lax.fori_loop(0, n * pairs, one, 0)
+        lax.fori_loop(begin * n * pairs // 4, end * n * pairs // 4, one, 0)
 
     load_w.wait()
     for p in range(2):
         wg[0, p, 0, 0, 0, mine] = own_w[p * PIECE:(p + 1) * PIECE, :].astype(jnp.bfloat16)
     pl.semaphore_wait(barrier, len(partners))
     gather_z(0)
-    choose()
-
-    stages = (
-        functools.partial(gather_m, 0),
-        functools.partial(gather_m, 1),
-        functools.partial(gather_l, 0),
-        functools.partial(gather_l, 1),
+
+    def prepare(begin, end):
+        if begin == 0:
+            choose()
+            load_x.wait()
+        turn(begin, end)
+
+    gather = [functools.partial(gather_m, 0), (0, 1), functools.partial(gather_l, 0)]
+    gather += [functools.partial(gather_m, k) for k in range(1, odd_group + 1) if k != 1 or groups[1]]
+    gather += [(1, 2)]
+    gather += [functools.partial(gather_l, k) for k in range(1, odd_group + 1) if k != 1 or groups[1]]
+    gather += [(2, 4)]
+    stages = gather + [
         gather_far,
         functools.partial(project, 0),
         functools.partial(project, 1),
         norm_1,
         norm_2,
         gradient,
-        reduce_z,
+        functools.partial(reduce_z, by_m[:-1]),
         functools.partial(reduce_2, ODD_0),
+        functools.partial(reduce_z, by_m[-1:]),
         functools.partial(reduce_2, EVEN_0),
+        functools.partial(reduce_2, AHEAD),
         functools.partial(reduce_2, EVEN_1),
-        functools.partial(reduce_3, 1),
-        functools.partial(reduce_3, 0),
+        reduce_3_odd,
+        reduce_3_ahead,
+        reduce_3_even,
         update,
-    )
+    ]
     for s in range(ITERS):
-        for i, stage in enumerate(stages):
-            if s == 0 and i == TURN_AT:
-                load_x.wait()
-                turn()
-            stage(s)
+        for stage in stages:
+            if not isinstance(stage, tuple):
+                stage(s)
+            elif s == 0:
+                prepare(*stage)
     for out in DEPARTURES:
         leave(out)
 

time: 117 us -> 109 us (0.932)
  Pallas kernels: 112 us -> 103 us
    pallas_call x1, Pallas kernels: 112 us -> 103 us  [on_device(): pl.pallas_call(functools.partial(kernel, dims, total_rows, math.sqrt(feat...]
where the time goes in v3:
time: 109 us; the launch traced here: 107 us
  Pallas kernels  103 us (94%)
  local copies, waits for them, and re-layouts  3.14 us (3%)
    pallas_call x1, Pallas kernels, on_device(): pl.pallas_call(functools.partial(kernel, dims, total_rows, math.sqrt(feat...  103 us
    unnamed x2, local copies, waits for them, and re-layouts  3.14 us

profile of v3, /device:TPU:0, one launch (start us, length us, event | category | flops | bytes accessed | tf_op | source)
XLA Modules:
  0.0 107.2 jit_solution(4127304044832751616)
XLA Ops:
  0.6 103.5 %cca_steps.1 = (f32[32,256]{1,0:T(8,128)}, bf16[768,256]{1,0:T(8,128)(2,1)}) custom-call(bf16[768,4096]{1,0:T(8,128)(2,1)} %bitcast.6, f32[32,256]{1,0:T(8,128)} %bitcast.7), custom_call_target="tpu_custom_call" | custom-call | flops 6442450944 | bytes 6291456 | tf_op jit(solution)/shard_map/cca_steps/pallas_call | solution.py:487
  104.1 1.4 %copy.6 = f32[1,32,256]{2,1,0:T(8,128)} copy(f32[1,32,256]{2,1,0:T(8,128)} %bitcast.5) | data formatting | bytes 65536
  105.5 1.8 %copy.7 = bf16[1,768,256]{2,1,0:T(8,128)(2,1)} copy(bf16[1,768,256]{2,1,0:T(8,128)(2,1)} %bitcast.4) | data formatting | bytes 786432
